TPU v7x, 32 devices: a whole 2x2x4 slice. The times are simulated.
32 devices in a mesh: dom: 8 (over z, y), agg: 4 (over x, core).
Axes of the slice: x: 2, y: 2, z: 4, core: 2. Of those that a mesh axis runs over, the one named last changes fastest.
Arguments:
- initial_guess: float32 [64, 262144], P(None, ('dom', 'agg')), may hold values from -6 to 6
- right_side: float32 [64, 262144], P(None, ('dom', 'agg')), may hold values from -6 to 6
- fine_tiles: bfloat16 [2048, 7, 128, 128], P(('dom', 'agg'))
- fine_smoother: bfloat16 [2048, 128, 128], P(('dom', 'agg'))
- fine_columns: int32 [2048, 7], P(('dom', 'agg')), may hold values from 0 to 71, as said below
- fine_sends: int32 [32, 8], P(('dom', 'agg')), may hold values from 0 to 63
- aggregate_map: int32 [262144], P(('dom', 'agg')), may hold values from 0 to 1023, as said below
- coarse_tiles: bfloat16 [256, 7, 128, 128], P('dom')
- coarse_smoother: bfloat16 [256, 128, 128], P('dom')
- coarse_columns: int32 [256, 7], P('dom'), may hold values from 0 to 39, as said below
- coarse_sends: int32 [8, 8], P('dom'), may hold values from 0 to 31
Outputs:
- smoothed: float32 [64, 262144], P(None, ('dom', 'agg'))
Inputs may be any that keep to these rules, and one draw needn't show every extreme that they name: `fine_columns`: in row block r of partition q, entry 0 is r, entries 1 to 3 are below 64, the last 3 entries are 64 or more. `coarse_columns`: in row block r of a group, entry 0 is r, entries 1 to 3 are below 32, the last 3 entries are 32 or more. `aggregate_map`: within each partition every value names exactly 8 of its rows; the rows of fine blocks 8 * c to 8 * c + 7 name values from c * 128 to c * 128 + 127.
All inputs are finite; a program needn't handle non-finite values.
Results may differ from a plain program's by a relative error of at most 0.02.
Values may be sent and summed in bfloat16 or wider, within the bound.
A program may use at most 128 MiB of HBM per device.

v0:
```python
import functools

import jax
import jax.numpy as jnp
from jax import lax
from jax.experimental import pallas as pl
from jax.experimental.pallas import tpu as pltpu
from jax.sharding import PartitionSpec as P

AGGR = 8
LOCAL = 4
BF = jnp.bfloat16
F32 = jnp.float32
MESH = pl.DeviceIdType.MESH
UNROLL = 8


def mm(a, b):
    return jnp.dot(a, b, preferred_element_type=F32)


def kernel(
    n,
    m,
    x_in,
    b_in,
    ft_in,
    fs_in,
    map_in,
    ct_in,
    cs_in,
    fc,
    fsend,
    cc,
    csend,
    out,
    stage,
    b,
    ft,
    fs,
    amap,
    ct,
    cs,
    x,
    xb,
    acc,
    member,
    send,
    ghost,
    e1,
    cb,
    e2,
    gath,
    lsem,
    tsem,
    ssem,
    rsem,
    gssem,
    grsem,
    osem,
):
    me = lax.axis_index("dom")
    ag = lax.axis_index("agg")
    own, systems, width = x.shape
    coarse = own // AGGR
    chunks = own // UNROLL
    split = LOCAL * width

    def lanes(r, count=1):
        return pl.ds(pl.multiple_of(r * width, width), count * width)

    load_x = pltpu.make_async_copy(x_in, stage, lsem.at[0])
    load_map = pltpu.make_async_copy(map_in, amap, lsem.at[1])
    load_b = pltpu.make_async_copy(b_in, b, lsem.at[2])
    load_fs = pltpu.make_async_copy(fs_in, fs, lsem.at[3])
    mine = pl.ds(ag * coarse, coarse)
    load_ct = pltpu.make_async_copy(ct_in.at[mine], ct, lsem.at[4])
    load_cs = pltpu.make_async_copy(cs_in.at[mine], cs, lsem.at[5])

    def load_tiles(c):
        rows = pl.ds(c * UNROLL, UNROLL)
        return pltpu.make_async_copy(ft_in.at[rows], ft.at[rows], tsem.at[c])

    load_x.start()
    load_map.start()
    load_b.start()
    for c in range(chunks):
        load_tiles(c).start()
    load_fs.start()
    load_ct.start()
    load_cs.start()

    barrier = pltpu.get_barrier_semaphore()
    for o in range(1, n):
        pl.semaphore_signal(
            barrier, inc=1, device_id=(lax.rem(me + o, n), ag), device_id_type=MESH
        )
    for o in range(1, m):
        pl.semaphore_signal(
            barrier, inc=1, device_id=(me, lax.rem(ag + o, m)), device_id_type=MESH
        )

    def exchange(e, table, rows_of):
        group = min(UNROLL, n)
        for first in range(1, n + 1, group):
            places = [lax.rem(me + o, n) for o in range(first, min(first + group, n + 1))]
            values = rows_of([table[0, d] for d in places])
            for i, (d, value) in enumerate(zip(places, values)):
                if first + i < n:
                    send[e, d] = value
                else:
                    ghost[e][d] = value
            for i, d in enumerate(places):
                if first + i < n:
                    pltpu.make_async_remote_copy(
                        src_ref=send.at[e, d],
                        dst_ref=ghost[e].at[me],
                        send_sem=ssem.at[e],
                        recv_sem=rsem.at[e],
                        device_id=(d, ag),
                        device_id_type=MESH,
                    ).start()

    def all_of(e):
        return pltpu.make_async_remote_copy(
            src_ref=send.at[e, pl.ds(0, n - 1)],
            dst_ref=ghost[e].at[pl.ds(0, n - 1)],
            send_sem=ssem.at[e],
            recv_sem=rsem.at[e],
            device_id=(lax.rem(me + 1, n), ag),
            device_id_type=MESH,
        )

    def ghost_part(e, r):
        near = ft.shape[1] // width
        parts = [ghost[e][jnp.maximum(fc[k, r] - own, 0)] for k in range(LOCAL, near)]
        return mm(jnp.concatenate(parts, axis=1), ft[r, split:, :])

    def local_phase(waits):
        @pl.loop(0, chunks)
        def _(c):
            if waits:
                load_tiles(c).wait()
            results = []
            for u in range(UNROLL):
                r = c * UNROLL + u
                parts = [xb[r]] + [xb[fc[k, r]] for k in range(1, LOCAL)]
                total = mm(jnp.concatenate(parts, axis=1), ft[r, :split, :])
                results.append(b[:, lanes(r)] - total)
            for u in range(UNROLL):
                acc[c * UNROLL + u] = results[u]

    def updated(e, rows):
        rest = [(acc[r] - ghost_part(e, r)).astype(BF) for r in rows]
        return [x[r] + mm(v, fs[r]) for r, v in zip(rows, rest)]

    def ghost_phase(e):
        @pl.loop(0, chunks)
        def _(c):
            rows = [c * UNROLL + u for u in range(UNROLL)]
            fresh = updated(e, rows)
            for r, v in zip(rows, fresh):
                x[r] = v
                xb[r] = v.astype(BF)

    def sweep(e, waits=False):
        local_phase(waits)
        if waits:
            load_fs.wait()
        all_of(e).wait_recv()
        exchange(e + 1, fsend, lambda rows: [v.astype(BF) for v in updated(e, rows)])
        ghost_phase(e)

    load_x.wait()

    @pl.loop(0, chunks)
    def _(c):
        for u in range(UNROLL):
            r = c * UNROLL + u
            v = stage[:, lanes(r)]
            x[r] = v
            xb[r] = v.astype(BF)

    pl.semaphore_wait(barrier, n - 1 + m - 1)
    exchange(0, fsend, lambda rows: [xb[r] for r in rows])

    load_map.wait()

    @pl.loop(0, own)
    def _(r):
        names = amap[pl.ds(r, 1), :] - (r // AGGR) * width
        wanted = lax.broadcasted_iota(jnp.int32, (width, width), 0)
        member[r] = jnp.where(names == wanted, 1.0, 0.0).astype(BF)

    load_b.wait()
    sweep(0, True)
    sweep(1)

    local_phase(False)
    load_ct.wait()
    load_cs.wait()
    all_of(2).wait_recv()

    @pl.loop(0, coarse)
    def _(c):
        rows = [c * AGGR + u for u in range(AGGR)]
        remain = [acc[r] - ghost_part(2, r) for r in rows]
        high = [v.astype(BF) for v in remain]
        low = [(v - h.astype(F32)).astype(BF) for v, h in zip(remain, high)]
        both = jnp.concatenate(
            [jnp.concatenate(high, axis=1), jnp.concatenate(low, axis=1)], axis=0
        )
        table = jnp.concatenate([member[r] for r in rows], axis=1)
        total = lax.dot_general(
            both, table, (((1,), (1,)), ((), ())), preferred_element_type=F32
        )
        kept = (total[:systems] + total[systems:]).astype(BF)
        cb[c] = kept
        first = mm(kept, cs[c])
        e1[c] = first
        gath[ag * coarse + c] = first.astype(BF)

    def gather_to(other, place):
        return pltpu.make_async_remote_copy(
            src_ref=gath.at[place],
            dst_ref=gath.at[place],
            send_sem=gssem.at[0],
            recv_sem=grsem.at[0],
            device_id=(me, other),
            device_id_type=MESH,
        )

    for o in range(1, m):
        gather_to(lax.rem(ag + o, m), mine).start()
    gather_all = gather_to(lax.rem(ag + 1, m), pl.ds(0, (m - 1) * coarse))
    gather_all.wait_recv()
    exchange(5, csend, lambda rows: [gath[r] for r in rows])
    left = []
    for j in range(coarse):
        r = ag * coarse + j
        parts = [gath[r]] + [gath[cc[k, r]] for k in range(1, LOCAL)]
        left.append(cb[j].astype(F32) - mm(jnp.concatenate(parts, axis=1), ct[j, :split, :]))
    for j in range(coarse):
        acc[j] = left[j]
    all_of(5).wait_recv()
    group = m * coarse
    rest = []
    for j in range(coarse):
        r = ag * coarse + j
        near = ct.shape[1] // width
        parts = [ghost[5][jnp.maximum(cc[k, r] - group, 0)] for k in range(LOCAL, near)]
        rest.append((acc[j] - mm(jnp.concatenate(parts, axis=1), ct[j, split:, :])).astype(BF))
    for j in range(coarse):
        second = e1[j] + mm(rest[j], cs[j])
        high = second.astype(BF)
        e2[j, :systems] = high
        e2[j, systems:] = (second - high.astype(F32)).astype(BF)

    def lifted(rows):
        both = [mm(e2[r // AGGR], member[r]) for r in rows]
        return [x[r] + (v[:systems] + v[systems:]) for r, v in zip(rows, both)]

    exchange(3, fsend, lambda rows: [v.astype(BF) for v in lifted(rows)])

    @pl.loop(0, chunks)
    def _(c):
        rows = [c * UNROLL + u for u in range(UNROLL)]
        fresh = lifted(rows)
        for r, v in zip(rows, fresh):
            x[r] = v
            xb[r] = v.astype(BF)

    sweep(3)
    local_phase(False)
    all_of(4).wait_recv()

    def store_out(c):
        place = lanes(c * UNROLL, UNROLL)
        return pltpu.make_async_copy(stage.at[:, place], out.at[:, place], osem.at[c])

    @pl.loop(0, chunks)
    def _(c):
        rows = [c * UNROLL + u for u in range(UNROLL)]
        fresh = updated(4, rows)
        for r, v in zip(rows, fresh):
            stage[:, lanes(r)] = v
        store_out(c).start()

    for e in range(6):
        all_of(e).wait_send()
    gather_all.wait_send()

    @pl.loop(0, chunks)
    def _(c):
        store_out(c).wait()


def shards(n, m, x, b, ft, fs, fc, fsend, amap, ct, cs, cc, csend):
    own, tiles, width, _ = ft.shape
    systems = x.shape[0]
    group = ct.shape[0]
    coarse = own // AGGR
    chunks = own // UNROLL
    hbm = pl.BlockSpec(memory_space=pl.ANY)
    smem = pl.BlockSpec(memory_space=pltpu.SMEM)
    block = (systems, width)
    return pl.pallas_call(
        functools.partial(kernel, n, m),
        out_shape=jax.ShapeDtypeStruct(x.shape, F32),
        in_specs=[hbm] * 7 + [smem] * 4,
        out_specs=hbm,
        scratch_shapes=[
            pltpu.VMEM(x.shape, F32),
            pltpu.VMEM(x.shape, F32),
            pltpu.VMEM((own, tiles * width, width), BF),
            pltpu.VMEM((own, width, width), BF),
            pltpu.VMEM((own, width), jnp.int32),
            pltpu.VMEM((coarse, tiles * width, width), BF),
            pltpu.VMEM((coarse, width, width), BF),
            pltpu.VMEM((own,) + block, F32),
            pltpu.VMEM((own,) + block, BF),
            pltpu.VMEM((own,) + block, F32),
            pltpu.VMEM((own, width, width), BF),
            pltpu.VMEM((6, n) + block, BF),
            [pltpu.VMEM((n,) + block, BF)] * 6,
            pltpu.VMEM((coarse,) + block, F32),
            pltpu.VMEM((coarse,) + block, BF),
            pltpu.VMEM((coarse, 2 * systems, width), BF),
            pltpu.VMEM((group,) + block, BF),
            pltpu.SemaphoreType.DMA((6,)),
            pltpu.SemaphoreType.DMA((chunks,)),
            pltpu.SemaphoreType.DMA((6,)),
            pltpu.SemaphoreType.DMA((6,)),
            pltpu.SemaphoreType.DMA((1,)),
            pltpu.SemaphoreType.DMA((1,)),
            pltpu.SemaphoreType.DMA((chunks,)),
        ],
        compiler_params=pltpu.CompilerParams(
            collective_id=0, has_side_effects=True, vmem_limit_bytes=60 * 1024 * 1024
        ),
        cost_estimate=pl.CostEstimate(
            flops=6_000_000_000, bytes_accessed=27_000_000, transcendentals=0
        ),
    )(
        x,
        b,
        ft.reshape(own, tiles * width, width),
        fs,
        amap.reshape(own, width),
        ct.reshape(group, tiles * width, width),
        cs,
        fc.T,
        fsend,
        cc.T,
        csend,
    )


def solution(mesh):
    return jax.shard_map(
        functools.partial(shards, mesh.shape["dom"], mesh.shape["agg"]),
        mesh=mesh,
        in_specs=(
            P(None, ("dom", "agg")),
            P(None, ("dom", "agg")),
            P(("dom", "agg"), None, None, None),
            P(("dom", "agg"), None, None),
            P(("dom", "agg"), None),
            P(("dom", "agg"), None),
            P(("dom", "agg")),
            P("dom", None, None, None),
            P("dom", None, None),
            P("dom", None),
            P("dom", None),
        ),
        out_specs=P(None, ("dom", "agg")),
        check_vma=False,
    )
```

profile of v0, /device:TPU:0, one launch (start us, length us, event | category | flops | bytes accessed | tf_op | source)
XLA Modules:
  0.0 58.3 jit_solution(15373492043396453432)
XLA Ops:
  0.0 55.2 %shard_map.109 = f32[64,8192]{1,0:T(8,128)} custom-call(f32[64,8192]{1,0:T(8,128)} %x_in.1, f32[64,8192]{1,0:T(8,128)} %b_in.1, bf16[64,896,128]{2,1,0:T(8,128)(2,1)} %bitcast.5, bf16[64,128,128]{2,1,0:T(8,128)(2,1)} %fs_in.1, s32[64,128]{1,0:T(8,128)} %bitcast.7, bf16[32,896,128]{2,1,0:T(8,128)(2,1)} %bitcast.6, bf16[32,128,128]{2,1,0:T(8,128)(2,1)} %cs_in.1, ...), custom_call_target="tpu_custom_call" | custom-call | flops 6000000000 | bytes 27000000 | tf_op jit(solution)/shard_map/pallas_call | solution.py:307
  55.2 3.1 %copy.13 = f32[64,8192]{1,0:T(8,128)} copy(f32[64,8192]{1,0:T(8,128)} %shard_map.109) | data formatting | bytes 4194304
where the time goes:
time: 58.5 us; the launch traced here: 58.3 us
  Pallas kernels  55.2 us (94%)
  local copies, waits for them, and re-layouts  3.06 us (5%)
    pallas_call x1, Pallas kernels, shards(): pl.pallas_call(functools.partial(kernel, n, m), out_shape=jax.ShapeDtypeS...  55.2 us
    unnamed x1, local copies, waits for them, and re-layouts  3.06 us

commit v1 on v0

--- a/solution.py
+++ b/solution.py
@@ -12,7 +12,8 @@
 BF = jnp.bfloat16
 F32 = jnp.float32
 MESH = pl.DeviceIdType.MESH
-UNROLL = 8
+UNROLL = 32
+PIECE = 8
 
 
 def mm(a, b):
@@ -64,6 +65,7 @@
     own, systems, width = x.shape
     coarse = own // AGGR
     chunks = own // UNROLL
+    pieces = own // PIECE
     split = LOCAL * width
 
     def lanes(r, count=1):
@@ -78,13 +80,13 @@
     load_cs = pltpu.make_async_copy(cs_in.at[mine], cs, lsem.at[5])
 
     def load_tiles(c):
-        rows = pl.ds(c * UNROLL, UNROLL)
+        rows = pl.ds(c * PIECE, PIECE)
         return pltpu.make_async_copy(ft_in.at[rows], ft.at[rows], tsem.at[c])
 
     load_x.start()
     load_map.start()
     load_b.start()
-    for c in range(chunks):
+    for c in range(pieces):
         load_tiles(c).start()
     load_fs.start()
     load_ct.start()
@@ -101,7 +103,7 @@
         )
 
     def exchange(e, table, rows_of):
-        group = min(UNROLL, n)
+        group = min(PIECE, n)
         for first in range(1, n + 1, group):
             places = [lax.rem(me + o, n) for o in range(first, min(first + group, n + 1))]
             values = rows_of([table[0, d] for d in places])
@@ -137,18 +139,17 @@
         return mm(jnp.concatenate(parts, axis=1), ft[r, split:, :])
 
     def local_phase(waits):
-        @pl.loop(0, chunks)
+        size = PIECE if waits else UNROLL
+
+        @pl.loop(0, own // size)
         def _(c):
             if waits:
                 load_tiles(c).wait()
-            results = []
-            for u in range(UNROLL):
-                r = c * UNROLL + u
+            for u in range(size):
+                r = c * size + u
                 parts = [xb[r]] + [xb[fc[k, r]] for k in range(1, LOCAL)]
                 total = mm(jnp.concatenate(parts, axis=1), ft[r, :split, :])
-                results.append(b[:, lanes(r)] - total)
-            for u in range(UNROLL):
-                acc[c * UNROLL + u] = results[u]
+                acc[r] = b[:, lanes(r)] - total
 
     def updated(e, rows):
         rest = [(acc[r] - ghost_part(e, r)).astype(BF) for r in rows]
@@ -173,10 +174,10 @@
 
     load_x.wait()
 
-    @pl.loop(0, chunks)
-    def _(c):
-        for u in range(UNROLL):
-            r = c * UNROLL + u
+    @pl.loop(0, pieces)
+    def _(c):
+        for u in range(PIECE):
+            r = c * PIECE + u
             v = stage[:, lanes(r)]
             x[r] = v
             xb[r] = v.astype(BF)
@@ -220,20 +221,28 @@
         e1[c] = first
         gath[ag * coarse + c] = first.astype(BF)
 
-    def gather_to(other, place):
+    def slab(owner):
+        return pl.ds(owner * coarse, coarse)
+
+    def gather_to(other, owner, slot):
         return pltpu.make_async_remote_copy(
-            src_ref=gath.at[place],
-            dst_ref=gath.at[place],
-            send_sem=gssem.at[0],
-            recv_sem=grsem.at[0],
+            src_ref=gath.at[slab(owner)],
+            dst_ref=gath.at[slab(owner)],
+            send_sem=gssem.at[slot],
+            recv_sem=grsem.at[slot],
             device_id=(me, other),
             device_id_type=MESH,
         )
 
-    for o in range(1, m):
-        gather_to(lax.rem(ag + o, m), mine).start()
-    gather_all = gather_to(lax.rem(ag + 1, m), pl.ds(0, (m - 1) * coarse))
-    gather_all.wait_recv()
+    mate = ag + 1 - 2 * lax.rem(ag, 2)
+    far = lax.rem(ag + 2, 4)
+    gathers = [gather_to(far, ag, 0), gather_to(mate, ag, 1), gather_to(mate, far, 2)]
+    gathers[0].start()
+    gathers[1].start()
+    gathers[0].wait_recv()
+    gathers[2].start()
+    gathers[1].wait_recv()
+    gathers[2].wait_recv()
     exchange(5, csend, lambda rows: [gath[r] for r in rows])
     left = []
     for j in range(coarse):
@@ -288,7 +297,8 @@
 
     for e in range(6):
         all_of(e).wait_send()
-    gather_all.wait_send()
+    for copy in gathers:
+        copy.wait_send()
 
     @pl.loop(0, chunks)
     def _(c):
@@ -301,6 +311,7 @@
     group = ct.shape[0]
     coarse = own // AGGR
     chunks = own // UNROLL
+    pieces = own // PIECE
     hbm = pl.BlockSpec(memory_space=pl.ANY)
     smem = pl.BlockSpec(memory_space=pltpu.SMEM)
     block = (systems, width)
@@ -328,11 +339,11 @@
             pltpu.VMEM((coarse, 2 * systems, width), BF),
             pltpu.VMEM((group,) + block, BF),
             pltpu.SemaphoreType.DMA((6,)),
-            pltpu.SemaphoreType.DMA((chunks,)),
+            pltpu.SemaphoreType.DMA((pieces,)),
             pltpu.SemaphoreType.DMA((6,)),
             pltpu.SemaphoreType.DMA((6,)),
-            pltpu.SemaphoreType.DMA((1,)),
-            pltpu.SemaphoreType.DMA((1,)),
+            pltpu.SemaphoreType.DMA((3,)),
+            pltpu.SemaphoreType.DMA((3,)),
             pltpu.SemaphoreType.DMA((chunks,)),
         ],
         compiler_params=pltpu.CompilerParams(

time: 58.5 us -> 53.4 us (0.913)
  Pallas kernels: 55.2 us -> 50.2 us
    pallas_call x1, Pallas kernels: 55.2 us -> 50.2 us  [shards(): pl.pallas_call(functools.partial(kernel, n, m), out_shape=jax.ShapeDtypeS...]
where the time goes in v1:
time: 53.4 us; the launch traced here: 53.3 us
  Pallas kernels  50.2 us (94%)
  local copies, waits for them, and re-layouts  3.06 us (6%)
    pallas_call x1, Pallas kernels, shards(): pl.pallas_call(functools.partial(kernel, n, m), out_shape=jax.ShapeDtypeS...  50.2 us
    unnamed x1, local copies, waits for them, and re-layouts  3.06 us

profile of v1, /device:TPU:0, one launch (start us, length us, event | category | flops | bytes accessed | tf_op | source)
XLA Modules:
  0.0 53.3 jit_solution(10128518428299441918)
XLA Ops:
  0.0 50.2 %shard_map.109 = f32[64,8192]{1,0:T(8,128)} custom-call(f32[64,8192]{1,0:T(8,128)} %x_in.1, f32[64,8192]{1,0:T(8,128)} %b_in.1, bf16[64,896,128]{2,1,0:T(8,128)(2,1)} %bitcast.5, bf16[64,128,128]{2,1,0:T(8,128)(2,1)} %fs_in.1, s32[64,128]{1,0:T(8,128)} %bitcast.7, bf16[32,896,128]{2,1,0:T(8,128)(2,1)} %bitcast.6, bf16[32,128,128]{2,1,0:T(8,128)(2,1)} %cs_in.1, ...), custom_call_target="tpu_custom_call" | custom-call | flops 6000000000 | bytes 27000000 | tf_op jit(solution)/shard_map/pallas_call | solution.py:318
  50.2 3.1 %copy.13 = f32[64,8192]{1,0:T(8,128)} copy(f32[64,8192]{1,0:T(8,128)} %shard_map.109) | data formatting | bytes 4194304

commit v2 on v1

--- a/solution.py
+++ b/solution.py
@@ -187,7 +187,7 @@
 
     load_map.wait()
 
-    @pl.loop(0, own)
+    @pl.loop(0, own, unroll=8)
     def _(r):
         names = amap[pl.ds(r, 1), :] - (r // AGGR) * width
         wanted = lax.broadcasted_iota(jnp.int32, (width, width), 0)
@@ -202,7 +202,7 @@
     load_cs.wait()
     all_of(2).wait_recv()
 
-    @pl.loop(0, coarse)
+    @pl.loop(0, coarse, unroll=4)
     def _(c):
         rows = [c * AGGR + u for u in range(AGGR)]
         remain = [acc[r] - ghost_part(2, r) for r in rows]

time: 53.4 us -> 53 us (level)
  no operation moved by 1% of the time
where the time goes in v2:
time: 53 us; the launch traced here: 52.8 us
  Pallas kernels  49.7 us (94%)
  local copies, waits for them, and re-layouts  3.06 us (6%)
    pallas_call x1, Pallas kernels, shards(): pl.pallas_call(functools.partial(kernel, n, m), out_shape=jax.ShapeDtypeS...  49.7 us
    unnamed x1, local copies, waits for them, and re-layouts  3.06 us

profile of v2, /device:TPU:0, one launch (start us, length us, event | category | flops | bytes accessed | tf_op | source)
XLA Modules:
  0.0 52.8 jit_solution(3923550573831968981)
XLA Ops:
  0.0 49.7 %shard_map.109 = f32[64,8192]{1,0:T(8,128)} custom-call(f32[64,8192]{1,0:T(8,128)} %x_in.1, f32[64,8192]{1,0:T(8,128)} %b_in.1, bf16[64,896,128]{2,1,0:T(8,128)(2,1)} %bitcast.5, bf16[64,128,128]{2,1,0:T(8,128)(2,1)} %fs_in.1, s32[64,128]{1,0:T(8,128)} %bitcast.7, bf16[32,896,128]{2,1,0:T(8,128)(2,1)} %bitcast.6, bf16[32,128,128]{2,1,0:T(8,128)(2,1)} %cs_in.1, ...), custom_call_target="tpu_custom_call" | custom-call | flops 6000000000 | bytes 27000000 | tf_op jit(solution)/shard_map/pallas_call | solution.py:318
  49.7 3.1 %copy.13 = f32[64,8192]{1,0:T(8,128)} copy(f32[64,8192]{1,0:T(8,128)} %shard_map.109) | data formatting | bytes 4194304
